TPU v7x, 32 devices: a whole 2x2x4 slice. The times are simulated.
32 devices in a mesh: island: 16 (over z, x, core), fsdp: 2 (over y).
Axes of the slice: x: 2, y: 2, z: 4, core: 2. Of those that a mesh axis runs over, the one named last changes fastest.
Arguments:
- hidden: bfloat16 [16, 256, 8192], P('island', 'fsdp'), may hold values from -6 to 6
- gain: bfloat16 [8192], P('fsdp'), may hold values from 0.5 to 1.5
- doc_ids: int32 [16, 256], P('island', 'fsdp'), may hold values from 0 to 7, never falling along the last dimension, each value on 1 to 64 neighbouring positions
- cotangent: bfloat16 [16, 256, 512], P('island', 'fsdp'), may hold values from -0.1796875 to 0.1796875
- pseudo_grad: bfloat16 [16, 8192, 512], P('island', 'fsdp'), may hold values from -0.375 to 0.375
- outer_weight: float32 [8192, 512], P(('fsdp', 'island')), may hold values from -0.0625 to 0.0625
- momentum: float32 [8192, 512], P(('fsdp', 'island')), may hold values from -0.0625 to 0.0625
Outputs:
- keys: bfloat16 [16, 256, 512], P('island', 'fsdp')
- grad_weight: bfloat16 [16, 8192, 512], P('island', 'fsdp')
- grad_gain: float32 [16, 8192], P('island', 'fsdp')
- new_outer: float32 [8192, 512], P(('fsdp', 'island'))
- new_momentum: float32 [8192, 512], P(('fsdp', 'island'))
Inputs may be any that keep to these rules, and one draw needn't show every extreme that they name: `doc_ids`: document numbers never fall along a replica's sequence; every document holds 1 to 64 tokens, and one holds exactly 64.
All inputs are finite; a program needn't handle non-finite values.
Results may differ from a plain program's by a relative error of at most 0.014.
Values may be sent and summed in bfloat16 or wider, within the bound.
A program may use at most 128 MiB of HBM per device.

v0:
```python
import math

import jax
import jax.numpy as jnp
from jax import lax
from jax.sharding import PartitionSpec as P

HEAD = 128
DOCS = 8


learn_rate = 0.7
momentum_rate = 0.9
norm_eps = 1e-05
rope_base = 500000.0
far_index = 1 << 30


def angles_for(positions, head_width):
    half_width = head_width // 2
    frequency = jnp.exp(
        jnp.arange(half_width, dtype=jnp.float32) * (-2.0 * math.log(rope_base) / head_width)
    )
    phases = positions[:, None] * frequency[None, :]
    return (jnp.cos(phases), jnp.sin(phases))


def rotate(values, cosine, sine_part, sign):
    rows = values.shape[0]
    half_width = cosine.shape[1]
    shaped = values.reshape(rows, -1, 2 * half_width)
    leading = shaped[:, :, :half_width]
    second = shaped[:, :, half_width:]
    cos_b = cosine[:, None, :]
    sin_b = sine_part[:, None, :] * sign
    joined = jnp.concatenate(
        [leading * cos_b - second * sin_b, second * cos_b + leading * sin_b], axis=2
    )
    return joined.reshape(rows, -1)


def body(hidden, gain, doc_ids, cotangent, pseudo_grad, outer_weight, momentum):
    islands = lax.axis_size("island")
    fsdp_ways = lax.axis_size("fsdp")
    summed = lax.psum_scatter(
        pseudo_grad[0].astype(jnp.float32), "island", scatter_dimension=0, tiled=True
    )
    mean_delta = summed / islands
    new_momentum = momentum_rate * momentum + mean_delta
    new_outer = outer_weight - learn_rate * (mean_delta + momentum_rate * new_momentum)
    fresh_rows = new_outer.astype(jnp.bfloat16)
    weight_shard = lax.all_gather(fresh_rows, "island", axis=0, tiled=True)
    tok_rows = hidden.shape[1]
    indices = lax.axis_index("fsdp") * tok_rows + jnp.arange(tok_rows, dtype=jnp.int32)
    documents = jnp.arange(DOCS, dtype=jnp.int32)
    in_document = doc_ids[0][:, None] == documents[None, :]
    local_first = jnp.min(jnp.where(in_document, indices[:, None], far_index), axis=0)
    starts = lax.pmin(local_first, "fsdp")
    doc_start = jnp.sum(jnp.where(in_document, starts[None, :], 0), axis=1)
    positions = (indices - doc_start).astype(jnp.float32)
    cosine, sine_part = angles_for(positions, HEAD)
    hidden_f = hidden[0].astype(jnp.float32)
    row_scale = lax.rsqrt(jnp.mean(hidden_f * hidden_f, axis=1, keepdims=True) + norm_eps)
    back_grad = rotate(cotangent[0].astype(jnp.float32), cosine, sine_part, -1.0).astype(
        jnp.bfloat16
    )
    columns = lax.all_to_all(hidden[0], "fsdp", split_axis=1, concat_axis=0, tiled=True)
    all_scales = lax.all_gather(row_scale, "fsdp", axis=0, tiled=True)
    normed_cols = columns.astype(jnp.float32) * all_scales
    act_cols = (normed_cols * gain.astype(jnp.float32)[None, :]).astype(jnp.bfloat16)
    weight_full, gain_full = (
        lax.all_gather(weight_shard, "fsdp", axis=0, tiled=True),
        lax.all_gather(gain, "fsdp", axis=0, tiled=True),
    )
    activations = (hidden_f * row_scale * gain_full.astype(jnp.float32)[None, :]).astype(
        jnp.bfloat16
    )
    projected = jnp.dot(activations, weight_full, preferred_element_type=jnp.float32)
    all_back = lax.all_gather(back_grad, "fsdp", axis=0, tiled=True)
    hidden_grad = lax.dot_general(
        all_back, weight_shard, (((1,), (1,)), ((), ())), preferred_element_type=jnp.float32
    )
    grad_gain = jnp.sum(hidden_grad * normed_cols, axis=0)
    grad_weight = jnp.zeros((act_cols.shape[1], all_back.shape[1]), jnp.float32)
    for block in range(fsdp_ways):
        act_block = act_cols[block * tok_rows : (block + 1) * tok_rows]
        back_block = all_back[block * tok_rows : (block + 1) * tok_rows]
        part = lax.dot_general(
            act_block, back_block, (((0,), (0,)), ((), ())), preferred_element_type=jnp.float32
        )
        grad_weight = grad_weight + part.astype(jnp.bfloat16).astype(jnp.float32)
    rotated = rotate(projected, cosine, sine_part, 1.0).astype(jnp.bfloat16)
    return (
        rotated[None],
        grad_weight.astype(jnp.bfloat16)[None],
        grad_gain[None],
        new_outer,
        new_momentum,
    )


def solution(mesh):
    placed = (
        P("island", "fsdp", None),
        P("fsdp"),
        P("island", "fsdp"),
        P("island", "fsdp", None),
        P("island", "fsdp", None),
        P(("fsdp", "island"), None),
        P(("fsdp", "island"), None),
    )
    return jax.shard_map(
        body,
        mesh=mesh,
        in_specs=placed,
        out_specs=(
            P("island", "fsdp", None),
            P("island", "fsdp", None),
            P("island", "fsdp"),
            P(("fsdp", "island"), None),
            P(("fsdp", "island"), None),
        ),
        check_vma=False,
    )
```

profile of v0, /device:TPU:0, one launch (start us, length us, event | category | flops | bytes accessed | tf_op | source)
XLA Modules:
  0.0 343.0 jit_solution(15746681793380100324)
XLA Ops:
  7.2 6.6 %bitcast_convert_fusion = f32[4096,512]{1,0:T(8,128)} fusion(bf16[1,4096,512]{2,1,0:T(8,128)(2,1)} %param.11), kind=kLoop, calls=%fused_computation.11 | loop fusion | flops 2097152 | bytes 12582912 | tf_op jit(solution)/shard_map/convert_element_type | solution.py:46
  13.9 107.5 %reduce-scatter.2.cloned.1.call-done = f32[256,512]{1,0:T(8,128)} async-done(((f32[4096,512]{1,0:T(8,128)}), f32[256,512]{1,0:T(8,128)}) %reduce-scatter.2.cloned.1.call-update) | async-done | bytes 524304 | tf_op jit(solution)/shard_map/reduce_scatter | solution.py:45
  121.4 2.3 fusion.15
  123.8 50.7 %all-gather.5.cloned.1.call-done = bf16[4096,512]{1,0:T(8,128)(2,1)} async-done(((bf16[256,512]{1,0:T(8,128)(2,1)}), bf16[4096,512]{1,0:T(8,128)(2,1)}) %all-gather.5.cloned.1.call-update) | async-done | bytes 4194320 | tf_op jit(solution)/shard_map/all_gather | solution.py:52
  174.6 2.8 all_to_all.10
  177.3 4.3 %copy.21 = bf16[128,2,4096]{2,0,1:T(8,128)(2,1)} copy(bf16[128,2,4096]{2,1,0:T(2,128)(2,1)} %all_to_all.10) | data formatting | bytes 4194304 | tf_op jit(solution)/shard_map/all_to_all | solution.py:67
  181.6 0.1 select_reduce_fusion.1
  181.8 4.0 %all-to-all-start = ((bf16[128,2,4096]{2,0,1:T(8,128)(2,1)}), bf16[128,2,4096]{2,0,1:T(8,128)(2,1)S(1)}, u32[]{:S(2)}, u32[]{:S(2)}) async-start(bf16[128,2,4096]{2,0,1:T(8,128)(2,1)} %copy.21), calls=%async_computation.1 | async-start | bytes 4194304 | tf_op jit(solution)/shard_map/all_to_all | solution.py:67
  185.7 48.3 %pmin.7 = s32[8]{0:T(128)S(1)} all-reduce(s32[8]{0:T(128)S(1)} %select_reduce_fusion.1), channel_id=1, replica_groups=mesh['island'=16,'fsdp'=2] {'fsdp'}, use_global_device_ids=true, to_apply=%region_3.4 | all-reduce | flops 8 | bytes 64 | tf_op jit(solution)/shard_map/pmin | solution.py:58
  234.0 4.5 %all_gather.15 = bf16[8192]{0:T(1024)(128)(2,1)S(1)} all-gather(bf16[4096]{0:T(1024)(128)(2,1)S(1)} %copy-done.5), channel_id=1, replica_groups=mesh['island'=16,'fsdp'=2] {'fsdp'}, dimensions={0}, use_global_device_ids=true | all-gather | bytes 24576 | tf_op jit(solution)/shard_map/all_gather | solution.py:73
  238.5 0.1 copy.22
  238.6 2.1 fusion.1
  240.7 4.2 %all-gather.1 = f32[2,1,128]{2,1,0:T(1,128)S(1)} all-gather(f32[1,1,128]{2,1,0:T(1,128)S(1)} %get-tuple-element.34), channel_id=2, replica_groups=mesh['island'=16,'fsdp'=2] {'fsdp'}, dimensions={0}, use_global_device_ids=true | all-gather | bytes 1536 | tf_op jit(solution)/shard_map/all_gather | solution.py:68
  245.0 0.2 broadcast_multiply_fusion
  245.3 1.3 copy-done
  246.6 4.4 %bitcast_multiply_fusion = (f32[256,4096]{1,0:T(8,128)}, bf16[256,4096]{1,0:T(8,128)(2,1)S(1)}) fusion(f32[256]{0:T(256)S(1)} %bitcast.34, bf16[128,2,4096]{2,0,1:T(8,128)(2,1)} %copy-done, f32[4096]{0:T(1024)S(1)} %convert_element_type.94), kind=kLoop, calls=%fused_computation.10 | loop fusion | flops 4194304 | bytes 8406016 | tf_op jit(solution)/shard_map/mul | solution.py:69
  251.0 50.4 %all-gather.7.cloned.1.call-done = bf16[8192,512]{1,0:T(8,128)(2,1)} async-done(((bf16[4096,512]{1,0:T(8,128)(2,1)}), bf16[8192,512]{1,0:T(8,128)(2,1)}) %all-gather.7.cloned.1.call-update) | async-done | bytes 8388624 | tf_op jit(solution)/shard_map/all_gather | solution.py:72
  301.3 11.8 %copy.20 = bf16[512,8192]{1,0:T(8,128)(2,1)} copy(bf16[512,8192]{0,1:T(8,128)(2,1)} %bitcast.28) | data formatting | bytes 16777216 | tf_op jit(solution)/shard_map/dot_general | solution.py:78
  313.1 6.4 %fusion.5 = f32[128,4,128]{0,2,1:T(8,128)S(1)} fusion(bf16[4,128,8192]{2,1,0:T(8,128)(2,1)} %bitcast.29, bf16[1,128,8192]{2,1,0:T(8,128)(2,1)} %param.7, f32[8192]{0:T(1024)S(1)} %convert_element_type.83, f32[128]{0:T(128)S(1)} %get-tuple-element.35), kind=kOutput, calls=%fused_computation.14 | convolution fusion | flops 1077936128 | bytes 10781184 | tf_op jit(solution)/shard_map/dot_general | solution.py:78
  319.6 6.1 %all_gather.19 = bf16[256,512]{0,1:T(8,128)(2,1)S(1)} all-gather(bf16[128,512]{0,1:T(8,128)(2,1)S(1)} %bitcast.31), channel_id=1, replica_groups=mesh['island'=16,'fsdp'=2] {'fsdp'}, dimensions={0}, use_global_device_ids=true | all-gather | bytes 393216 | tf_op jit(solution)/shard_map/all_gather | solution.py:79
  325.7 1.3 convolution_convert_fusion
  327.0 3.3 fusion
  330.3 0.8 copy.23
  331.1 5.4 %fusion.9 = f32[4096]{0:T(1024)} fusion(f32[256,4096]{1,0:T(8,128)} %get-tuple-element.23, bf16[256,512]{0,1:T(8,128)(2,1)S(1)} %all_gather.19, bf16[4096,512]{1,0:T(8,128)(2,1)} %all-gather.5.cloned.1.call-done), kind=kOutput, calls=%fused_computation.17 | convolution fusion | flops 1075834880 | bytes 8667136 | tf_op jit(solution)/shard_map/dot_general | solution.py:80
  (30 shorter events, 0.4 us)
Async XLA Ops:
  7.2 114.3 %reduce-scatter.2.cloned.1.call-start = ((), (), s32[]{:S(2)}) async-start(), calls=%async_computation.2 | async-start | bytes 8912896 | tf_op jit(solution)/shard_map/reduce_scatter | solution.py:45
  13.8 107.6 %copy-start.2 = (f32[256,512]{1,0:T(8,128)S(1)}, f32[256,512]{1,0:T(8,128)}, u32[]{:S(2)}) copy-start(f32[256,512]{1,0:T(8,128)} %param.12) | copy-start | bytes 1572868
  13.8 107.6 %copy-start.3 = (f32[256,512]{1,0:T(8,128)S(1)}, f32[256,512]{1,0:T(8,128)}, u32[]{:S(2)}) copy-start(f32[256,512]{1,0:T(8,128)} %param.13) | copy-start | bytes 1572868
  13.9 160.7 %copy-start.1 = (bf16[1,128,8192]{2,1,0:T(8,128)(2,1)S(1)}, bf16[1,128,8192]{2,1,0:T(8,128)(2,1)}, u32[]{:S(2)}) copy-start(bf16[1,128,8192]{2,1,0:T(8,128)(2,1)} %param.7) | copy-start | bytes 6291460
  13.9 160.6 %all-gather.5.cloned.1.call-start = ((), (), s32[]{:S(2)}) async-start(), calls=%async_computation.3 | async-start | bytes 4456448 | tf_op jit(solution)/shard_map/all_gather | solution.py:52
  123.7 177.6 %all-gather.7.cloned.1.call-start = ((), (), s32[]{:S(2)}) async-start(), calls=%async_computation.4 | async-start | bytes 12582912 | tf_op jit(solution)/shard_map/all_gather | solution.py:72
  174.5 7.1 %copy-start.6 = (s32[1,128]{1,0:T(1,128)S(1)}, s32[1,128]{1,0:T(1,128)}, u32[]{:S(2)}) copy-start(s32[1,128]{1,0:T(1,128)} %param.9) | copy-start | bytes 1540
  177.3 56.7 %copy-start.5 = (bf16[4096]{0:T(1024)(128)(2,1)S(1)}, bf16[4096]{0:T(1024)(128)(2,1)}, u32[]{:S(2)}) copy-start(bf16[4096]{0:T(1024)(128)(2,1)} %param.8) | copy-start | bytes 24580
  177.3 61.2 %copy-start.4 = (bf16[1,128,512]{2,1,0:T(8,128)(2,1)S(1)}, bf16[1,128,512]{2,1,0:T(8,128)(2,1)}, u32[]{:S(2)}) copy-start(bf16[1,128,512]{2,1,0:T(8,128)(2,1)} %param.10) | copy-start | bytes 393220
  181.8 63.5 %all-to-all-start = ((bf16[128,2,4096]{2,0,1:T(8,128)(2,1)}), bf16[128,2,4096]{2,0,1:T(8,128)(2,1)S(1)}, u32[]{:S(2)}, u32[]{:S(2)}) async-start(bf16[128,2,4096]{2,0,1:T(8,128)(2,1)} %copy.21), calls=%async_computation.1 | async-start | bytes 4194304 | tf_op jit(solution)/shard_map/all_to_all | solution.py:67
  245.2 1.3 copy-start
Sparse Core Ops, SparseCore 0:
  14.0 107.4 reduce-scatter.1
  124.2 50.3 all-gather.4
  176.1 125.2 all-gather.6
where the time goes:
time: 344 us; the launch traced here: 343 us
  waiting for transfers between devices  209 us (61%)
  blocking collectives  63 us (18%)
  local copies, waits for them, and re-layouts  21 us (6%)
  matrix products  16.4 us (5%)
  other arithmetic  15.9 us (5%)
  between operations  13.9 us (4%)
  starting transfers between devices  4.08 us (1%)
    reduce_scatter x1, waiting for transfers between devices, body(): lax.psum_scatter(pseudo_grad[0].astype(jnp.float32), 'island', scatter_di...  108 us
    all_gather x1, waiting for transfers between devices, body(): weight_shard = lax.all_gather(fresh_rows, 'island', axis=0, tiled=True)  50.7 us
    all_gather x1, waiting for transfers between devices, body(): lax.all_gather(weight_shard, 'fsdp', axis=0, tiled=True)  50.4 us
    pmin x1, blocking collectives, body(): starts = lax.pmin(local_first, 'fsdp')  48.3 us
    dot_general x1, local copies, waits for them, and re-layouts, body(): jnp.dot(activations, weight_full, preferred_element_type=jnp.float32)  11.8 us
    all_to_all x2, local copies, waits for them, and re-layouts, body(): lax.all_to_all(hidden[0], 'fsdp', split_axis=1, concat_axis=0, tiled=True)  7.07 us
  transfers between devices with their start and end apart: 4, of which 3 were waited for; matrix products, arithmetic and copies ran while one was open for 3% of the time, Pallas kernels for 0%

commit v1 on v0

v1 whole, which is shorter than its diff:
```python
import functools
import math

import jax
import jax.numpy as jnp
from jax import lax
from jax.experimental import pallas as pl
from jax.experimental.pallas import tpu as pltpu
from jax.sharding import PartitionSpec as P

HEAD = 128
DOCS = 8


learn_rate = 0.7
momentum_rate = 0.9
norm_eps = 1e-05
rope_base = 500000.0
far_index = 1 << 30


def angles_for(positions, head_width):
    half_width = head_width // 2
    frequency = jnp.exp(
        jnp.arange(half_width, dtype=jnp.float32) * (-2.0 * math.log(rope_base) / head_width)
    )
    phases = positions[:, None] * frequency[None, :]
    return (jnp.cos(phases), jnp.sin(phases))


def rotate(values, cosine, sine_part, sign):
    rows = values.shape[0]
    half_width = cosine.shape[1]
    shaped = values.reshape(rows, -1, 2 * half_width)
    leading = shaped[:, :, :half_width]
    second = shaped[:, :, half_width:]
    cos_b = cosine[:, None, :]
    sin_b = sine_part[:, None, :] * sign
    joined = jnp.concatenate(
        [leading * cos_b - second * sin_b, second * cos_b + leading * sin_b], axis=2
    )
    return joined.reshape(rows, -1)


def exchange_kernel(islands, ways, stages, chunks, *refs):
    (delta, outer, mom, hidden, cot, scale, docs) = refs[:7]
    (weight, new_outer, new_mom, cols, all_cot, all_scale, all_docs) = refs[7:14]
    scratch = list(refs[14:])
    recv = [scratch.pop(0) for _ in range(stages)]
    send = [None] + [scratch.pop(0) for _ in range(stages - 1)]
    kept = [None] + [scratch.pop(0) for _ in range(stages - 1)]
    rs_send, rs_recv, ag_send, ag_recv, f_send, f_recv, local_sem = scratch

    me = lax.axis_index("island")
    way = lax.axis_index("fsdp")
    bits = [me // (1 << k) % 2 for k in range(stages)]
    partners = [me + (1 - 2 * bits[k]) * (1 << k) for k in range(stages)]
    rows = outer.shape[0]
    step = rows // chunks
    width = hidden.shape[1] // ways

    barrier = pltpu.get_barrier_semaphore()
    for k in range(stages):
        pl.semaphore_signal(
            barrier, inc=1, device_id={"island": partners[k]},
            device_id_type=pl.DeviceIdType.MESH,
        )
    for d in range(1, ways):
        pl.semaphore_signal(
            barrier, inc=1, device_id={"fsdp": lax.rem(way + d, ways)},
            device_id_type=pl.DeviceIdType.MESH,
        )
    pl.semaphore_wait(barrier, stages + ways - 1)

    def halving(k, c):
        part = pl.ds(c * step, step)
        src = delta.at[:, 1 - bits[0], part] if k == 0 else send[k].at[:, part]
        return pltpu.make_async_remote_copy(
            src_ref=src, dst_ref=recv[k].at[:, part],
            send_sem=rs_send.at[k, c], recv_sem=rs_recv.at[k, c],
            device_id={"island": partners[k]}, device_id_type=pl.DeviceIdType.MESH,
        )

    def doubling(k, c):
        part = pl.ds(c * step, step)
        span = 1 << (k + 1)
        low = lax.rem(me, span)
        copies = []
        for j in range(islands // span):
            slot = islands - islands // (1 << k) + j
            copies.append(pltpu.make_async_remote_copy(
                src_ref=weight.at[j * span + low, part],
                dst_ref=weight.at[j * span + low, part],
                send_sem=ag_send.at[c, slot], recv_sem=ag_recv.at[c, slot],
                device_id={"island": partners[k]}, device_id_type=pl.DeviceIdType.MESH,
            ))
        return copies

    for c in range(chunks):
        halving(0, c).start()

    pieces = ((cols, None), (all_cot, cot), (all_scale, scale), (all_docs, docs))

    def across(d):
        to = lax.rem(way + d, ways)
        copies = []
        for i, (dst, src) in enumerate(pieces):
            if src is None:
                src = hidden.at[:, pl.ds(pl.multiple_of(to * width, width), width)]
            copies.append(pltpu.make_async_remote_copy(
                src_ref=src, dst_ref=dst.at[way],
                send_sem=f_send.at[d - 1, i], recv_sem=f_recv.at[d - 1, i],
                device_id={"fsdp": to}, device_id_type=pl.DeviceIdType.MESH,
            ))
        return copies

    for d in range(1, ways):
        for copy in across(d):
            copy.start()
    own = []
    for i, (dst, src) in enumerate(pieces):
        if src is None:
            src = hidden.at[:, pl.ds(pl.multiple_of(way * width, width), width)]
        own.append(pltpu.make_async_copy(src, dst.at[way], local_sem.at[i]))
    for copy in own:
        copy.start()

    def reduce_stage(k, c):
        part = pl.ds(c * step, step)
        halving(k, c).wait_recv()

        def total(m):
            mine = delta[m, bits[0], part] if k == 0 else kept[k][m, part]
            return mine.astype(jnp.float32) + recv[k][m, part].astype(jnp.float32)

        if k < stages - 1:
            count = islands >> (k + 2)

            def to_send(j, carry):
                send[k + 1][j, part] = total(2 * j + 1 - bits[k + 1]).astype(jnp.bfloat16)
                return carry

            def to_keep(j, carry):
                kept[k + 1][j, part] = total(2 * j + bits[k + 1])
                return carry

            lax.fori_loop(0, count, to_send, 0)
            halving(k + 1, c).start()
            lax.fori_loop(0, count, to_keep, 0)
        else:
            mean_delta = total(0) / islands
            fresh_mom = momentum_rate * mom[part] + mean_delta
            fresh = outer[part] - learn_rate * (mean_delta + momentum_rate * fresh_mom)
            weight[me, part] = fresh.astype(jnp.bfloat16)
            for copy in doubling(stages - 1, c):
                copy.start()
            new_mom[part] = fresh_mom
            new_outer[part] = fresh

    def gather_stage(k, c):
        for copy in doubling(k, c):
            copy.wait_recv()
        if k > 0:
            for copy in doubling(k - 1, c):
                copy.start()

    for tick in range(2 * stages + chunks - 1):
        for c in range(chunks):
            k = tick - c
            if 0 <= k < stages:
                reduce_stage(k, c)
            elif stages <= k < 2 * stages:
                gather_stage(2 * stages - 1 - k, c)

    for c in range(chunks):
        for k in range(stages):
            halving(k, c).wait_send()
            for copy in doubling(k, c):
                copy.wait_send()
    for d in range(1, ways):
        for copy in across(d):
            copy.wait()
    for copy in own:
        copy.wait()


def exchange(delta, outer, mom, hidden, cot, scale, docs):
    islands = lax.axis_size("island")
    ways = lax.axis_size("fsdp")
    stages = islands.bit_length() - 1
    rows, width = outer.shape
    chunks = 4 if rows % 64 == 0 else 1
    tok, feats = hidden.shape
    bf, f32 = jnp.bfloat16, jnp.float32
    recv = [pltpu.VMEM((islands >> (k + 1), rows, width), bf) for k in range(stages)]
    send = [pltpu.VMEM((islands >> (k + 1), rows, width), bf) for k in range(1, stages)]
    kept = [pltpu.VMEM((islands >> (k + 1), rows, width), f32) for k in range(1, stages)]
    dma = pltpu.SemaphoreType.DMA
    vmem = pl.BlockSpec(memory_space=pltpu.VMEM)
    return pl.pallas_call(
        functools.partial(exchange_kernel, islands, ways, stages, chunks),
        out_shape=(
            jax.ShapeDtypeStruct((islands, rows, width), bf),
            jax.ShapeDtypeStruct((rows, width), f32),
            jax.ShapeDtypeStruct((rows, width), f32),
            jax.ShapeDtypeStruct((ways, tok, feats // ways), bf),
            jax.ShapeDtypeStruct((ways, tok, width), bf),
            jax.ShapeDtypeStruct((ways,) + scale.shape, f32),
            jax.ShapeDtypeStruct((ways,) + docs.shape, jnp.int32),
        ),
        in_specs=[vmem] * 7,
        out_specs=[vmem] * 7,
        scratch_shapes=recv + send + kept + [
            dma((stages, chunks)), dma((stages, chunks)),
            dma((chunks, islands)), dma((chunks, islands)),
            dma((max(ways - 1, 1), 4)), dma((max(ways - 1, 1), 4)), dma((4,)),
        ],
        compiler_params=pltpu.CompilerParams(
            collective_id=0, has_side_effects=True, vmem_limit_bytes=56 * 1024 * 1024
        ),
    )(delta.reshape(islands // 2, 2, rows, width), outer, mom, hidden, cot, scale, docs)


def body(hidden, gain, doc_ids, cotangent, pseudo_grad, outer_weight, momentum):
    fsdp_ways = lax.axis_size("fsdp")
    tok_rows = hidden.shape[1]
    hidden_f = hidden[0].astype(jnp.float32)
    row_scale = lax.rsqrt(jnp.mean(hidden_f * hidden_f, axis=1, keepdims=True) + norm_eps)
    weight, new_outer, new_momentum, columns, all_cot, all_scales, all_docs = exchange(
        pseudo_grad[0], outer_weight, momentum, hidden[0], cotangent[0],
        jnp.broadcast_to(row_scale, (tok_rows, 128)),
        jnp.broadcast_to(doc_ids, (8, tok_rows)),
    )
    weight = weight.reshape(-1, weight.shape[2])
    seq = fsdp_ways * tok_rows
    docs = all_docs[:, 0, :].reshape(seq)
    indices = jnp.arange(seq, dtype=jnp.int32)
    documents = jnp.arange(DOCS, dtype=jnp.int32)
    in_document = docs[:, None] == documents[None, :]
    starts = jnp.min(jnp.where(in_document, indices[:, None], far_index), axis=0)
    doc_start = jnp.sum(jnp.where(in_document, starts[None, :], 0), axis=1)
    positions = (indices - doc_start).astype(jnp.float32)
    cosine, sine_part = angles_for(positions, HEAD)
    all_back = rotate(
        all_cot.reshape(seq, -1).astype(jnp.float32), cosine, sine_part, -1.0
    ).astype(jnp.bfloat16)
    normed_cols = (
        columns.reshape(seq, -1).astype(jnp.float32) * all_scales[:, :, :1].reshape(seq, 1)
    )
    act_cols = (normed_cols * gain.astype(jnp.float32)[None, :]).astype(jnp.bfloat16)
    partial_proj = jnp.dot(act_cols, weight, preferred_element_type=jnp.float32)
    own = lax.axis_index("fsdp")
    if fsdp_ways == 2:
        other = lax.dynamic_slice_in_dim(partial_proj, (1 - own) * tok_rows, tok_rows, 0)
        mine = lax.dynamic_slice_in_dim(partial_proj, own * tok_rows, tok_rows, 0)
        got = lax.ppermute(other.astype(jnp.bfloat16), "fsdp", [(0, 1), (1, 0)])
        projected = mine + got.astype(jnp.float32)
    else:
        projected = lax.psum_scatter(partial_proj, "fsdp", scatter_dimension=0, tiled=True)
    hidden_grad = lax.dot_general(
        all_back, weight, (((1,), (1,)), ((), ())), preferred_element_type=jnp.float32
    )
    grad_gain = jnp.sum(hidden_grad * normed_cols, axis=0)
    grad_weight = jnp.zeros((act_cols.shape[1], all_back.shape[1]), jnp.float32)
    for block in range(fsdp_ways):
        act_block = act_cols[block * tok_rows : (block + 1) * tok_rows]
        back_block = all_back[block * tok_rows : (block + 1) * tok_rows]
        part = lax.dot_general(
            act_block, back_block, (((0,), (0,)), ((), ())), preferred_element_type=jnp.float32
        )
        grad_weight = grad_weight + part.astype(jnp.bfloat16).astype(jnp.float32)
    cos_own = lax.dynamic_slice_in_dim(cosine, own * tok_rows, tok_rows, 0)
    sin_own = lax.dynamic_slice_in_dim(sine_part, own * tok_rows, tok_rows, 0)
    rotated = rotate(projected, cos_own, sin_own, 1.0).astype(jnp.bfloat16)
    return (
        rotated[None],
        grad_weight.astype(jnp.bfloat16)[None],
        grad_gain[None],
        new_outer,
        new_momentum,
    )


def solution(mesh):
    placed = (
        P("island", "fsdp", None),
        P("fsdp"),
        P("island", "fsdp"),
        P("island", "fsdp", None),
        P("island", "fsdp", None),
        P(("fsdp", "island"), None),
        P(("fsdp", "island"), None),
    )
    return jax.shard_map(
        body,
        mesh=mesh,
        in_specs=placed,
        out_specs=(
            P("island", "fsdp", None),
            P("island", "fsdp", None),
            P("island", "fsdp"),
            P(("fsdp", "island"), None),
            P(("fsdp", "island"), None),
        ),
        check_vma=False,
    )
```

time: 344 us -> 105 us (0.31)
  waiting for transfers between devices: 209 us -> 0.01 us
  Pallas kernels: 0 us -> 75.3 us
  blocking collectives: 63 us -> 0 us
  local copies, waits for them, and re-layouts: 21 us -> 6.81 us
  between operations: 13.9 us -> 0.9 us
  matrix products: 16.4 us -> 7.72 us
  other arithmetic: 15.9 us -> 10.2 us
    reduce_scatter x1 -> x0, waiting for transfers between devices: 108 us -> none  [body(): lax.psum_scatter(pseudo_grad[0].astype(jnp.float32), 'island', scatter_di...]
    all_gather x2 -> x0, waiting for transfers between devices: 101 us -> none  [the longest x1 50.7 us: body(): weight_shard = lax.all_gather(fresh_rows, 'island', axis=0, tiled=True)]
    pallas_call x0 -> x1, Pallas kernels: none -> 75.3 us  [exchange(): pl.pallas_call(functools.partial(exchange_kernel, islands, ways, stages,...]
    pmin x1 -> x0, blocking collectives: 48.3 us -> none  [body(): starts = lax.pmin(local_first, 'fsdp')]
    all_gather x3 -> x0, blocking collectives: 14.8 us -> none  [the longest x1 6.05 us: body(): all_back = lax.all_gather(back_grad, 'fsdp', axis=0, tiled=True)]
    dot_general x1 -> x0, local copies, waits for them, and re-layouts: 11.8 us -> none  [body(): jnp.dot(activations, weight_full, preferred_element_type=jnp.float32)]
    dot_general x2, matrix products: 11.8 us -> 3.15 us  [the longest x1 1.92 us: body(): lax.dot_general(all_back, weight, (((1,), (1,)), ((), ())), preferred_ele...]
    all_to_all x2 -> x0, local copies, waits for them, and re-layouts: 7.07 us -> none  [body(): lax.all_to_all(hidden[0], 'fsdp', split_axis=1, concat_axis=0, tiled=True)]
  transfers between devices with their start and end apart: 4 -> 1, of which waited for: 3 -> 0; matrix products, arithmetic and copies ran while one was open for 3% -> 11% of each run, Pallas kernels for 0% -> 0%
where the time goes in v1:
time: 105 us
  Pallas kernels  75.3 us (72%)
  other arithmetic  10.2 us (10%)
  matrix products  7.72 us (7%)
  local copies, waits for them, and re-layouts  6.81 us (6%)
  starting transfers between devices  3.76 us (4%)
    pallas_call x1, Pallas kernels, exchange(): pl.pallas_call(functools.partial(exchange_kernel, islands, ways, stages,...  75.3 us
    dot_general x2, matrix products, body(): lax.dot_general(act_block, back_block, (((0,), (0,)), ((), ())), preferre...  4.57 us
    ppermute x1, starting transfers between devices, body(): got = lax.ppermute(other.astype(jnp.bfloat16), 'fsdp', [(0, 1), (1, 0)])  3.76 us
    convert_element_type x1, other arithmetic, body(): (normed_cols * gain.astype(jnp.float32)[None, :]).astype(jnp.bfloat16)  2.37 us
  transfers between devices with their start and end apart: 1, of which 0 were waited for; matrix products, arithmetic and copies ran while one was open for 11% of the time, Pallas kernels for 0%

profile of v1, /device:TPU:0, one launch (start us, length us, event | category | flops | bytes accessed | tf_op | source)
XLA Modules:
  0.0 104.7 jit_solution(5009691902321947303)
XLA Ops:
  0.6 2.1 %multiply_reduce_fusion = f32[128]{0:T(128)S(1)} fusion(bf16[1,128,8192]{2,1,0:T(8,128)(2,1)} %param.7), kind=kLoop, calls=%fused_computation.8 | loop fusion | flops 3145600 | bytes 2097664 | tf_op jit(solution)/shard_map/reduce_sum | solution.py:228
  2.7 0.7 broadcast_in_dim.34.refs_5_
  3.5 1.2 %broadcast_in_dim.56.refs_6_ = s32[8,128]{1,0:T(8,128)} broadcast(s32[128]{0:T(128)} %bitcast.44), dimensions={1} | broadcast | bytes 4608 | tf_op jit(solution)/shard_map/broadcast_in_dim | solution.py:232
  4.7 75.3 %shard_map.110 = (bf16[16,256,512]{2,1,0:T(8,128)(2,1)}, f32[256,512]{1,0:T(8,128)}, f32[256,512]{1,0:T(8,128)}, bf16[2,128,4096]{2,1,0:T(8,128)(2,1)}, bf16[2,1...) custom-call(bf16[8,2,256,512]{3,2,1,0:T(8,128)(2,1)} %bitcast.32, f32[256,512]{1,0:T(8,128)} %refs_1_.1, ...), custom_call_target="tpu_custom_call" | custom-call | tf_op jit(solution)/shard_map/pallas_call | solution.py:200
  80.0 1.0 slice_reduce_fusion
  81.0 2.4 %multiply_convert_fusion.1 = bf16[2,128,4096]{2,1,0:T(8,128)(2,1)S(1)} fusion(f32[4096]{0:T(1024)S(1)} %convert_element_type.84, f32[2,128]{1,0:T(2,128)S(1)} %slice_reduce_fusion, bf16[2,128,4096]{2,1,0:T(8,128)(2,1)} %get-tuple-element.12), kind=kLoop, calls=%fused_computation.7 | loop fusion | flops 4194304 | bytes 4211712 | tf_op jit(solution)/shard_map/convert_element_type | solution.py:250
  83.4 0.4 copy-done.1
  83.9 1.2 %fusion.11 = f32[256,512]{1,0:T(8,128)S(1)} fusion(bf16[256,4096]{1,0:T(8,128)(2,1)S(1)} %bitcast.36, bf16[4096,512]{1,0:T(8,128)(2,1)S(1)} %bitcast.33), kind=kOutput, calls=%fused_computation.39 | convolution fusion | flops 1073741824 | bytes 6815744 | tf_op jit(solution)/shard_map/dot_general | solution.py:251
  85.1 3.8 %collective-permute-start = (bf16[128,512]{1,0:T(8,128)(2,1)S(1)}, bf16[128,512]{1,0:T(8,128)(2,1)}, u32[]{:S(2)}, u32[]{:S(2)}) collective-permute-start(bf16[128,512]{1,0:T(8,128)(2,1)S(1)} %dynamic-slice_convert_fusion), channel_id=1, source_target_pairs={{0,1},{1,0},{2,3},{3,2},{4,5},{5,4},{6,7},{7,6},{8,9},{9,8},{10,11... | collective-permute-start | bytes 393224 | tf_op jit(solution)/shard_map/ppermute | solution.py:256
  88.9 0.5 multiply_exponential_fusion
  89.4 0.7 slice.38
  90.3 0.6 subtract_convert_fusion.1
  91.1 1.7 %bitcast_multiply_fusion = (f32[256,4096]{1,0:T(8,128)S(1)}, bf16[256,4096]{1,0:T(8,128)(2,1)S(1)}) fusion(f32[256]{0:T(256)} %bitcast.41, bf16[2,128,4096]{2,1,0:T(8,128)(2,1)S(1)} %copy-done, f32[4096]{0:T(1024)S(1)} %convert_element_type.84), kind=kLoop, calls=%fused_computation.5 | loop fusion | flops 4194304 | bytes 8406016 | tf_op jit(solution)/shard_map/mul | solution.py:248
  92.8 0.5 broadcast_multiply_fusion
  93.3 0.5 multiply_subtract_fusion
  93.8 0.4 maximum_convert_fusion
  94.3 1.9 %fusion.1 = f32[4096]{0:T(1024)} fusion(f32[256,4096]{1,0:T(8,128)S(1)} %get-tuple-element.19, bf16[4096,512]{1,0:T(8,128)(2,1)S(1)} %bitcast.34, bf16[32,8,4,128]{3,2,1,0:T(4,128)(2,1)S(1)} %bitcast.35), kind=kOutput, calls=%fused_computation.9 | convolution fusion | flops 1075834880 | bytes 8667136 | tf_op jit(solution)/shard_map/dot_general | solution.py:260
  96.2 1.3 %convolution_convert_fusion = bf16[4096,512]{1,0:T(8,128)(2,1)S(1)} fusion(bf16[256,4096]{1,0:T(8,128)(2,1)S(1)} %get-tuple-element.20, bf16[16,8,4,128]{3,2,1,0:T(4,128)(2,1)S(1)} %bitcast.38), kind=kOutput, calls=%fused_computation.1 | convolution fusion | flops 538968064 | bytes 5373952 | tf_op jit(solution)/shard_map/dot_general | solution.py:268
  97.5 3.3 %fusion = bf16[1,4096,512]{2,1,0:T(8,128)(2,1)} fusion(bf16[4096,512]{1,0:T(8,128)(2,1)S(1)} %convolution_convert_fusion, bf16[256,4096]{1,0:T(8,128)(2,1)S(1)} %get-tuple-element.20, bf16[16,8,4,128]{3,2,1,0:T(4,128)(2,1)S(1)} %bitcast.37), kind=kOutput, calls=%fused_computation.4 | convolution fusion | flops 547356672 | bytes 9568256 | tf_op jit(solution)/shard_map/dot_general | solution.py:268
  100.8 1.0 convert_add_fusion
  101.9 0.3 subtract_convert_fusion
  102.4 0.7 convert_element_type.90
  103.1 0.8 copy.29
  103.9 0.8 copy.30
  (30 shorter events, 0.8 us)
Async XLA Ops:
  2.7 78.3 %copy-start.7 = (bf16[4096]{0:T(1024)(128)(2,1)S(1)}, bf16[4096]{0:T(1024)(128)(2,1)}, u32[]{:S(2)}) copy-start(bf16[4096]{0:T(1024)(128)(2,1)} %param.8) | copy-start | bytes 24580
  81.0 2.4 %copy-start.6 = (f32[2,128]{1,0:T(2,128)}, f32[2,128]{1,0:T(2,128)S(1)}, u32[]{:S(2)}) copy-start(f32[2,128]{1,0:T(2,128)S(1)} %slice_reduce_fusion) | copy-start | bytes 3076
  81.0 2.8 %copy-start.1 = (bf16[16,256,512]{2,1,0:T(8,128)(2,1)S(1)}, bf16[16,256,512]{2,1,0:T(8,128)(2,1)}, u32[]{:S(2)}) copy-start(bf16[16,256,512]{2,1,0:T(8,128)(2,1)} %get-tuple-element.14) | copy-start | bytes 12582916
  83.4 7.5 %copy-start.5 = (bf16[2,128,512]{2,1,0:T(8,128)(2,1)S(1)}, bf16[2,128,512]{2,1,0:T(8,128)(2,1)}, u32[]{:S(2)}) copy-start(bf16[2,128,512]{2,1,0:T(8,128)(2,1)} %get-tuple-element.16) | copy-start | bytes 786436
  83.9 7.2 %copy-start = (bf16[2,128,4096]{2,1,0:T(8,128)(2,1)S(1)}, bf16[2,128,4096]{2,1,0:T(8,128)(2,1)}, u32[]{:S(2)}) copy-start(bf16[2,128,4096]{2,1,0:T(8,128)(2,1)} %get-tuple-element.12) | copy-start | bytes 6291460
  85.1 15.7 %collective-permute-start = (bf16[128,512]{1,0:T(8,128)(2,1)S(1)}, bf16[128,512]{1,0:T(8,128)(2,1)}, u32[]{:S(2)}, u32[]{:S(2)}) collective-permute-start(bf16[128,512]{1,0:T(8,128)(2,1)S(1)} %dynamic-slice_convert_fusion), channel_id=1, source_target_pairs={{0,1},{1,0},{2,3},{3,2},{4,5},{5,4},{6,7},{7,6},{8,9},{9,8},{10,11... | collective-permute-start | bytes 393224 | tf_op jit(solution)/shard_map/ppermute | solution.py:256
  91.1 1.7 %copy-start.8 = (f32[256]{0:T(256)S(1)}, f32[256]{0:T(256)}, u32[]{:S(2)}) copy-start(f32[256]{0:T(256)} %subtract_convert_fusion.1) | copy-start | bytes 3076
  91.1 1.7 %copy-start.9 = (f32[64]{0:T(128)S(1)}, f32[64]{0:T(128)}, u32[]{:S(2)}) copy-start(f32[64]{0:T(128)} %multiply_exponential_fusion) | copy-start | bytes 772
  91.1 3.2 %copy-start.2 = (bf16[16,256,512]{2,1,0:T(8,128)(2,1)S(1)}, bf16[16,256,512]{2,1,0:T(8,128)(2,1)}, u32[]{:S(2)}) copy-start(bf16[16,256,512]{2,1,0:T(8,128)(2,1)} %get-tuple-element.14) | copy-start | bytes 12582916
  97.5 5.6 %copy-start.4 = (f32[256,512]{1,0:T(8,128)S(1)}, f32[256,512]{1,0:T(8,128)}, u32[]{:S(2)}) copy-start(f32[256,512]{1,0:T(8,128)} %get-tuple-element.40) | copy-start | bytes 1572868
  100.8 3.1 %copy-start.3 = (f32[256,512]{1,0:T(8,128)S(1)}, f32[256,512]{1,0:T(8,128)}, u32[]{:S(2)}) copy-start(f32[256,512]{1,0:T(8,128)} %get-tuple-element.41) | copy-start | bytes 1572868

commit v2 on v1

v2 whole, which is shorter than its diff:
```python
import functools
import math

import jax
import jax.numpy as jnp
from jax import lax
from jax.experimental import pallas as pl
from jax.experimental.pallas import tpu as pltpu
from jax.sharding import PartitionSpec as P

HEAD = 128
DOCS = 8


learn_rate = 0.7
momentum_rate = 0.9
norm_eps = 1e-05
rope_base = 500000.0
far_index = 1 << 30


def turn(values, cosine, sine):
    heads = [values[:, i : i + HEAD] for i in range(0, values.shape[1], HEAD)]
    return jnp.concatenate(
        [head * cosine + pltpu.roll(head, HEAD // 2, 1) * sine for head in heads], axis=1
    )


CHUNKS = 4


def orders_for(stages, chunk):
    return list(range(stages))


def exchange_kernel(islands, ways, stages, chunks, *refs):
    (delta, outer, mom, hidden, cot, docs, gain) = refs[:7]
    (weight, new_outer, new_mom, act, back, keys) = refs[7:13]
    (cols, all_cot, info, all_info, part_out, part_in, angles) = refs[13:20]
    scratch = list(refs[20:])
    recv = [scratch.pop(0) for _ in range(stages)]
    send = [None] + [scratch.pop(0) for _ in range(stages - 1)]
    kept = [None] + [scratch.pop(0) for _ in range(stages - 1)]
    rs_send, rs_recv, ag_send, ag_recv, f_send, f_recv, local_sem, p_send, p_recv = scratch
    tok = cot.shape[0]

    me = lax.axis_index("island")
    way = lax.axis_index("fsdp")
    bits = [me // (1 << k) % 2 for k in range(stages)]
    partners = [me + (1 - 2 * bits[k]) * (1 << k) for k in range(stages)]
    rows = outer.shape[0]
    step = rows // chunks
    width = hidden.shape[1] // ways

    barrier = pltpu.get_barrier_semaphore()
    for k in range(stages):
        pl.semaphore_signal(
            barrier, inc=1, device_id={"island": partners[k]},
            device_id_type=pl.DeviceIdType.MESH,
        )
    for d in range(1, ways):
        pl.semaphore_signal(
            barrier, inc=1, device_id={"fsdp": lax.rem(way + d, ways)},
            device_id_type=pl.DeviceIdType.MESH,
        )
    pl.semaphore_wait(barrier, stages + ways - 1)

    orders = [orders_for(stages, c) for c in range(chunks)]

    def halving(k, c):
        part = pl.ds(c * step, step)
        bit = orders[c][k]
        src = delta.at[:, 1 - bits[0], part] if k == 0 else send[k].at[:, part]
        return pltpu.make_async_remote_copy(
            src_ref=src, dst_ref=recv[k].at[:, part],
            send_sem=rs_send.at[k, c], recv_sem=rs_recv.at[k, c],
            device_id={"island": partners[bit]}, device_id_type=pl.DeviceIdType.MESH,
        )

    def doubling(k, c):
        part = pl.ds(c * step, step)
        bit = orders[c][k]
        fixed = sum(bits[b] * (1 << b) for b in orders[c][: k + 1])
        copies = []
        for j in range(islands >> (k + 1)):
            slot = islands - islands // (1 << k) + j
            block = fixed + sum((j >> i & 1) << b for i, b in enumerate(orders[c][k + 1 :]))
            copies.append(pltpu.make_async_remote_copy(
                src_ref=weight.at[block, part], dst_ref=weight.at[block, part],
                send_sem=ag_send.at[c, slot], recv_sem=ag_recv.at[c, slot],
                device_id={"island": partners[bit]}, device_id_type=pl.DeviceIdType.MESH,
            ))
        return copies

    for c in range(chunks):
        halving(0, c).start()

    pieces = ((cols, None), (all_cot, cot), (all_info, info))

    def across(d):
        to = lax.rem(way + d, ways)
        copies = []
        for i, (dst, src) in enumerate(pieces):
            if src is None:
                src = hidden.at[:, pl.ds(pl.multiple_of(to * width, width), width)]
            copies.append(pltpu.make_async_remote_copy(
                src_ref=src, dst_ref=dst.at[way],
                send_sem=f_send.at[d - 1, i], recv_sem=f_recv.at[d - 1, i],
                device_id={"fsdp": to}, device_id_type=pl.DeviceIdType.MESH,
            ))
        return copies

    for d in range(1, ways):
        for copy in across(d)[:2]:
            copy.start()
    own = []
    for i, (dst, src) in enumerate(pieces):
        if src is None:
            src = hidden.at[:, pl.ds(pl.multiple_of(way * width, width), width)]
        own.append(pltpu.make_async_copy(src, dst.at[way], local_sem.at[i]))
    for copy in own[:2]:
        copy.start()

    tile = 512

    def cut(i):
        return pl.ds(pl.multiple_of(i * tile, tile), tile)

    def norms():
        def add(i, total):
            block = hidden[:, cut(i)].astype(jnp.float32)
            block = block * block
            for lane in range(0, tile, HEAD):
                total = total + block[:, lane : lane + HEAD]
            return total

        squares = lax.fori_loop(
            0, hidden.shape[1] // tile, add, jnp.zeros((tok, HEAD), jnp.float32)
        )
        mean = jnp.sum(squares, axis=1, keepdims=True) / hidden.shape[1]
        info[0] = jnp.broadcast_to(lax.rsqrt(mean + norm_eps), (tok, HEAD))
        row = docs[...].astype(jnp.float32)
        info[1] = jnp.broadcast_to(row, (HEAD, tok)).T
        for d in range(1, ways):
            across(d)[2].start()
        own[2].start()

    def arrivals():
        for d in range(1, ways):
            for copy in across(d):
                copy.wait_recv()
        for copy in own:
            copy.wait()

    def find_angles():
        shape = (tok, HEAD)
        lane = lax.broadcasted_iota(jnp.int32, shape, 1)
        first_half = lane < HEAD // 2
        half_lane = jnp.where(first_half, lane, lane - HEAD // 2).astype(jnp.float32)
        frequency = jnp.exp(half_lane * (-2.0 * math.log(rope_base) / HEAD))
        token = lax.broadcasted_iota(jnp.int32, shape, 0).astype(jnp.float32)
        starts = []
        for s in range(DOCS):
            first = jnp.full((1, HEAD), float(far_index), jnp.float32)
            for f in range(ways):
                at = jnp.where(all_info[f, 1] == float(s), token + f * tok, float(far_index))
                first = jnp.minimum(first, jnp.min(at, axis=0, keepdims=True))
            starts.append(first)
        for f in range(ways):
            start = jnp.zeros(shape, jnp.float32)
            for s in range(DOCS):
                start = start + jnp.where(all_info[f, 1] == float(s), starts[s], 0.0)
            phases = (token + f * tok - start) * frequency
            sine = jnp.sin(phases)
            angles[f, 0] = jnp.cos(phases)
            angles[f, 1] = jnp.where(first_half, sine, -sine)

    def turn_back():
        for f in range(ways):
            back[pl.ds(f * tok, tok)] = turn(
                all_cot[f].astype(jnp.float32), angles[f, 0], angles[f, 1]
            ).astype(jnp.bfloat16)

    def activate(f):
        scale = all_info[f, 0][:, :1]

        def one(i, carry):
            normed = cols[f, :, cut(i)].astype(jnp.float32) * scale
            act[pl.ds(f * tok, tok), cut(i)] = (normed * gain[:, cut(i)]).astype(jnp.bfloat16)
            return carry

        lax.fori_loop(0, width // tile, one, 0)

    work = [arrivals, find_angles, turn_back]
    work += [functools.partial(activate, f) for f in range(ways)]

    def reduce_stage(k, c):
        part = pl.ds(c * step, step)
        halving(k, c).wait_recv()

        def total(m):
            mine = delta[m, bits[0], part] if k == 0 else kept[k][m, part]
            return mine.astype(jnp.float32) + recv[k][m, part].astype(jnp.float32)

        if k < stages - 1:
            count = islands >> (k + 2)
            following = orders[c][k + 1]
            below = 1 << sorted(orders[c][k + 1 :]).index(following)

            def place(j, bit):
                return j // below * (2 * below) + bit * below + j % below

            def to_send(j, carry):
                send[k + 1][j, part] = total(place(j, 1 - bits[following])).astype(jnp.bfloat16)
                return carry

            def to_keep(j, carry):
                kept[k + 1][j, part] = total(place(j, bits[following]))
                return carry

            lax.fori_loop(0, count, to_send, 0)
            halving(k + 1, c).start()
            lax.fori_loop(0, count, to_keep, 0)
        else:
            mean_delta = total(0) / islands
            fresh_mom = momentum_rate * mom[part] + mean_delta
            fresh = outer[part] - learn_rate * (mean_delta + momentum_rate * fresh_mom)
            weight[me, part] = fresh.astype(jnp.bfloat16)
            for copy in doubling(stages - 1, c):
                copy.start()
            new_mom[part] = fresh_mom
            new_outer[part] = fresh

    def gather_stage(k, c):
        for copy in doubling(k, c):
            copy.wait_recv()
        if k > 0:
            for copy in doubling(k - 1, c):
                copy.start()

    for tick in range(2 * stages + chunks - 1):
        for c in range(chunks):
            k = tick - c
            if 0 <= k < stages:
                reduce_stage(k, c)
                if tick == 1 and c == 0:
                    norms()
            elif stages <= k < 2 * stages:
                if work:
                    work.pop(0)()
                gather_stage(2 * stages - 1 - k, c)

    while work:
        work.pop(0)()

    def product(f):
        tokens = act[pl.ds(pl.multiple_of(f * tok, tok), tok), :]
        whole = weight[...].reshape(width, cot.shape[1])
        return jnp.dot(tokens, whole, preferred_element_type=jnp.float32)

    def swap(d):
        return pltpu.make_async_remote_copy(
            src_ref=part_out.at[d - 1], dst_ref=part_in.at[d - 1],
            send_sem=p_send.at[d - 1], recv_sem=p_recv.at[d - 1],
            device_id={"fsdp": lax.rem(way + d, ways)},
            device_id_type=pl.DeviceIdType.MESH,
        )

    for d in range(1, ways):
        part_out[d - 1] = product(lax.rem(way + d, ways)).astype(jnp.bfloat16)
        swap(d).start()
    projected = product(way)
    for c in range(chunks):
        for k in range(stages):
            halving(k, c).wait_send()
            for copy in doubling(k, c):
                copy.wait_send()
    for d in range(1, ways):
        for copy in across(d):
            copy.wait_send()
    for d in range(1, ways):
        swap(d).wait_recv()
        projected = projected + part_in[d - 1].astype(jnp.float32)
    keys[...] = turn(projected, angles[way, 0], -angles[way, 1]).astype(jnp.bfloat16)
    for d in range(1, ways):
        swap(d).wait_send()


def exchange(delta, outer, mom, hidden, cot, docs, gain):
    islands = lax.axis_size("island")
    ways = lax.axis_size("fsdp")
    stages = islands.bit_length() - 1
    rows, width = outer.shape
    chunks = CHUNKS if rows % (16 * CHUNKS) == 0 else 1
    tok, feats = hidden.shape
    bf, f32 = jnp.bfloat16, jnp.float32
    recv = [pltpu.VMEM((islands >> (k + 1), rows, width), bf) for k in range(stages)]
    send = [pltpu.VMEM((islands >> (k + 1), rows, width), bf) for k in range(1, stages)]
    kept = [pltpu.VMEM((islands >> (k + 1), rows, width), f32) for k in range(1, stages)]
    dma = pltpu.SemaphoreType.DMA
    vmem = pl.BlockSpec(memory_space=pltpu.VMEM)
    return pl.pallas_call(
        functools.partial(exchange_kernel, islands, ways, stages, chunks),
        out_shape=(
            jax.ShapeDtypeStruct((islands, rows, width), bf),
            jax.ShapeDtypeStruct((rows, width), f32),
            jax.ShapeDtypeStruct((rows, width), f32),
            jax.ShapeDtypeStruct((ways * tok, feats // ways), bf),
            jax.ShapeDtypeStruct((ways * tok, width), bf),
            jax.ShapeDtypeStruct((tok, width), bf),
        ),
        in_specs=[vmem] * 7,
        out_specs=[vmem] * 6,
        scratch_shapes=[
            pltpu.VMEM((ways, tok, feats // ways), bf),
            pltpu.VMEM((ways, tok, width), bf),
            pltpu.VMEM((2, tok, HEAD), f32),
            pltpu.VMEM((ways, 2, tok, HEAD), f32),
            pltpu.VMEM((max(ways - 1, 1), tok, width), bf),
            pltpu.VMEM((max(ways - 1, 1), tok, width), bf),
            pltpu.VMEM((ways, 2, tok, HEAD), f32),
        ] + recv + send + kept + [
            dma((stages, chunks)), dma((stages, chunks)),
            dma((chunks, islands)), dma((chunks, islands)),
            dma((max(ways - 1, 1), 3)), dma((max(ways - 1, 1), 3)), dma((3,)),
            dma((max(ways - 1, 1),)), dma((max(ways - 1, 1),)),
        ],
        compiler_params=pltpu.CompilerParams(
            collective_id=0, has_side_effects=True, vmem_limit_bytes=56 * 1024 * 1024
        ),
    )(delta.reshape(islands // 2, 2, rows, width), outer, mom, hidden, cot, docs, gain)


def gradient_kernel(act, back, weight, gain, keys, outer, mom, *outs):
    (grad_weight, grad_gain, keys_out, outer_out, mom_out) = outs
    grad = lax.dot_general(
        act[...], back[...], (((0,), (0,)), ((), ())), preferred_element_type=jnp.float32
    )
    grad_weight[...] = grad.astype(jnp.bfloat16)
    ones = jnp.ones((8, grad.shape[1]), jnp.float32)
    sums = lax.dot_general(
        ones, grad * weight[...].astype(jnp.float32), (((1,), (1,)), ((), ())),
        precision=lax.Precision.HIGHEST, preferred_element_type=jnp.float32,
    )
    grad_gain[...] = sums[:1] / gain[...]
    keys_out[...] = keys[...]
    outer_out[...] = outer[...]
    mom_out[...] = mom[...]


def gradients(act, back, weight, gain, keys, outer, mom):
    seq, feats = act.shape
    width = back.shape[1]
    tiles = feats // 512

    def rows_of(array):
        return pl.BlockSpec((array.shape[0] // tiles, width), lambda i: (i, 0))

    row = pl.BlockSpec((1, 512), lambda i: (0, i))
    shape = jax.ShapeDtypeStruct
    return pl.pallas_call(
        gradient_kernel,
        grid=(tiles,),
        in_specs=[
            pl.BlockSpec((seq, 512), lambda i: (0, i)),
            pl.BlockSpec((seq, width), lambda i: (0, 0)),
            rows_of(weight), row, rows_of(keys), rows_of(outer), rows_of(mom),
        ],
        out_specs=[rows_of(weight), row, rows_of(keys), rows_of(outer), rows_of(mom)],
        out_shape=[
            shape(weight.shape, jnp.bfloat16), shape((1, feats), jnp.float32),
            shape(keys.shape, keys.dtype), shape(outer.shape, outer.dtype),
            shape(mom.shape, mom.dtype),
        ],
        compiler_params=pltpu.CompilerParams(vmem_limit_bytes=32 * 1024 * 1024),
    )(act, back, weight, gain, keys, outer, mom)


def body(hidden, gain, doc_ids, cotangent, pseudo_grad, outer_weight, momentum):
    gain_row = gain.astype(jnp.float32)[None, :]
    weight, new_outer, new_momentum, act, back, keys = exchange(
        pseudo_grad[0], outer_weight, momentum, hidden[0], cotangent[0], doc_ids, gain_row
    )
    grad_weight, grad_gain, keys, new_outer, new_momentum = gradients(
        act, back, weight.reshape(-1, weight.shape[2]), gain_row, keys, new_outer, new_momentum
    )
    return keys[None], grad_weight[None], grad_gain, new_outer, new_momentum


def solution(mesh):
    placed = (
        P("island", "fsdp", None),
        P("fsdp"),
        P("island", "fsdp"),
        P("island", "fsdp", None),
        P("island", "fsdp", None),
        P(("fsdp", "island"), None),
        P(("fsdp", "island"), None),
    )
    return jax.shard_map(
        body,
        mesh=mesh,
        in_specs=placed,
        out_specs=(
            P("island", "fsdp", None),
            P("island", "fsdp", None),
            P("island", "fsdp"),
            P(("fsdp", "island"), None),
            P(("fsdp", "island"), None),
        ),
        check_vma=False,
    )
```

time: 105 us -> 103 us (0.981)
  Pallas kernels: 75.3 us -> 92 us
  other arithmetic: 10.2 us -> 1.3 us
  matrix products: 7.72 us -> 0 us
  starting transfers between devices: 3.76 us -> 0 us
    pallas_call x0 -> x1, Pallas kernels: none -> 11 us  [gradients(): pl.pallas_call(gradient_kernel, grid=(tiles,), in_specs=[pl.BlockSpec((se...]
    dot_general x4 -> x0, matrix products: 7.72 us -> none  [the longest x2 4.57 us: body(): lax.dot_general(act_block, back_block, (((0,), (0,)), ((), ())), preferre...]
    pallas_call x1, Pallas kernels: 75.3 us -> 81 us  [exchange(): pl.pallas_call(functools.partial(exchange_kernel, islands, ways, stages,...]
    unnamed x22 -> x14, local copies, waits for them, and re-layouts: 2.05 us -> 7.71 us
    ppermute x1 -> x0, starting transfers between devices: 3.76 us -> none  [body(): got = lax.ppermute(other.astype(jnp.bfloat16), 'fsdp', [(0, 1), (1, 0)])]
    convert_element_type x4 -> x0, other arithmetic: 3.3 us -> none  [the longest x1 2.37 us: body(): (normed_cols * gain.astype(jnp.float32)[None, :]).astype(jnp.bfloat16)]
    mul x2 -> x0, other arithmetic: 2.19 us -> none  [the longest x1 1.66 us: body(): columns.reshape(seq, -1).astype(jnp.float32)]
    reduce_sum x2 -> x0, other arithmetic: 2.16 us -> none  [the longest x1 2.08 us: body(): jnp.mean(hidden_f * hidden_f, axis=1, keepdims=True) + norm_eps]
  transfers between devices with their start and end apart: 1 -> 0, of which waited for: 0 -> 0; matrix products, arithmetic and copies ran while one was open for 11% -> 0% of each run, Pallas kernels for 0% -> 0%
where the time goes in v2:
time: 103 us; the launch traced here: 102 us
  Pallas kernels  92 us (89%)
  local copies, waits for them, and re-layouts  7.71 us (7%)
  other arithmetic  1.3 us (1%)
    pallas_call x1, Pallas kernels, exchange(): pl.pallas_call(functools.partial(exchange_kernel, islands, ways, stages,...  81 us
    pallas_call x1, Pallas kernels, gradients(): pl.pallas_call(gradient_kernel, grid=(tiles,), in_specs=[pl.BlockSpec((se...  11 us
    unnamed x14, local copies, waits for them, and re-layouts  7.71 us

profile of v2, /device:TPU:0, one launch (start us, length us, event | category | flops | bytes accessed | tf_op | source)
XLA Modules:
  0.0 101.7 jit_solution(2638743554679004971)
XLA Ops:
  0.6 1.3 %broadcast_in_dim.15 = f32[4096]{0:T(1024)} convert(bf16[4096]{0:T(1024)(128)(2,1)} %param.8) | non-fusion elementwise | flops 4096 | bytes 24576 | tf_op jit(solution)/shard_map/broadcast_in_dim | solution.py:380
  1.9 0.0 copy-start.5
  1.9 81.0 %shard_map.110 = (bf16[16,256,512]{2,1,0:T(8,128)(2,1)}, f32[256,512]{1,0:T(8,128)}, f32[256,512]{1,0:T(8,128)}, bf16[256,4096]{1,0:T(8,128)(2,1)}, bf16[256,512]{1,0:T(8,128)(2,1)}, /*index=5*/bf16[128,512]{1,0:T(8,128)(2,1)}) custom-call(bf16[8,2,256,512]{3,2,1,0:T(8,128)(2,1)} %bitcast.10, f32[256,512]{1,0:T(8,128)} %refs_1_.1, f32[256,512]{1,0:T(8,128)} %refs_2_.1, ...), custom_call_target="tpu_custom_call" | custom-call | tf_op jit(solution)/shard_map/pallas_call | solution.py:302
  83.0 0.0 copy-done.5
  83.0 0.0 copy-start
  83.0 2.2 %copy-done = bf16[16,256,512]{2,1,0:T(8,128)(2,1)S(1)} copy-done((bf16[16,256,512]{2,1,0:T(8,128)(2,1)S(1)}, bf16[16,256,512]{2,1,0:T(8,128)(2,1)}, u32[]{:S(2)}) %copy-start) | copy-done | bytes 4194328
  85.2 0.0 copy-start.1
  85.2 1.6 %copy-done.1 = bf16[256,4096]{1,0:T(8,128)(2,1)S(1)} copy-done((bf16[256,4096]{1,0:T(8,128)(2,1)S(1)}, bf16[256,4096]{1,0:T(8,128)(2,1)}, u32[]{:S(2)}) %copy-start.1) | copy-done | bytes 2097176
  86.8 0.0 copy-start.2
  86.8 1.0 %copy-done.2 = f32[256,512]{1,0:T(8,128)S(1)} copy-done((f32[256,512]{1,0:T(8,128)S(1)}, f32[256,512]{1,0:T(8,128)}, u32[]{:S(2)}) %copy-start.2) | copy-done | bytes 524312
  87.8 0.0 copy-start.3
  87.8 1.0 %copy-done.3 = f32[256,512]{1,0:T(8,128)S(1)} copy-done((f32[256,512]{1,0:T(8,128)S(1)}, f32[256,512]{1,0:T(8,128)}, u32[]{:S(2)}) %copy-start.3) | copy-done | bytes 524312
  88.8 0.0 copy-start.4
  88.9 0.9 copy-done.4
  89.8 0.0 copy-start.6
  89.8 0.9 copy-done.6
  90.7 11.0 %shard_map.111 = (bf16[4096,512]{1,0:T(8,128)(2,1)}, f32[1,4096]{1,0:T(1,128)}, bf16[128,512]{1,0:T(8,128)(2,1)}, f32[256,512]{1,0:T(8,128)}, f32[256,512]{1,0:T(8,128)}) custom-call(bf16[256,4096]{1,0:T(8,128)(2,1)S(1)} %copy-done.1, bf16[256,512]{1,0:T(8,128)(2,1)S(1)} %copy-done.4, bf16[4096,512]{1,0:T(8,128)(2,1)S(1)} %bitcast.7, f32[1,4096]{1,0:T(1,128)S(1)} %bitcast.9, ...), custom_call_target="tpu_custom_call" | custom-call | tf_op jit(solution)/shard_map/pallas_call | solution.py:361
Async XLA Ops:
  1.9 81.0 %copy-start.5 = (f32[4096]{0:T(1024)S(1)}, f32[4096]{0:T(1024)}, u32[]{:S(2)}) copy-start(f32[4096]{0:T(1024)} %broadcast_in_dim.15) | copy-start | bytes 49156
  83.0 2.2 %copy-start = (bf16[16,256,512]{2,1,0:T(8,128)(2,1)S(1)}, bf16[16,256,512]{2,1,0:T(8,128)(2,1)}, u32[]{:S(2)}) copy-start(bf16[16,256,512]{2,1,0:T(8,128)(2,1)} %get-tuple-element.18) | copy-start | bytes 12582916
  85.2 1.6 %copy-start.1 = (bf16[256,4096]{1,0:T(8,128)(2,1)S(1)}, bf16[256,4096]{1,0:T(8,128)(2,1)}, u32[]{:S(2)}) copy-start(bf16[256,4096]{1,0:T(8,128)(2,1)} %get-tuple-element.16.act) | copy-start | bytes 6291460
  86.8 1.0 %copy-start.2 = (f32[256,512]{1,0:T(8,128)S(1)}, f32[256,512]{1,0:T(8,128)}, u32[]{:S(2)}) copy-start(f32[256,512]{1,0:T(8,128)} %get-tuple-element.20.outer) | copy-start | bytes 1572868
  87.8 1.0 %copy-start.3 = (f32[256,512]{1,0:T(8,128)S(1)}, f32[256,512]{1,0:T(8,128)}, u32[]{:S(2)}) copy-start(f32[256,512]{1,0:T(8,128)} %get-tuple-element.21.mom) | copy-start | bytes 1572868
  88.8 0.9 copy-start.4
  89.8 0.9 copy-start.6

commit v3 on v2

--- a/solution.py
+++ b/solution.py
@@ -331,59 +331,19 @@
     )(delta.reshape(islands // 2, 2, rows, width), outer, mom, hidden, cot, docs, gain)
 
 
-def gradient_kernel(act, back, weight, gain, keys, outer, mom, *outs):
-    (grad_weight, grad_gain, keys_out, outer_out, mom_out) = outs
-    grad = lax.dot_general(
-        act[...], back[...], (((0,), (0,)), ((), ())), preferred_element_type=jnp.float32
-    )
-    grad_weight[...] = grad.astype(jnp.bfloat16)
-    ones = jnp.ones((8, grad.shape[1]), jnp.float32)
-    sums = lax.dot_general(
-        ones, grad * weight[...].astype(jnp.float32), (((1,), (1,)), ((), ())),
-        precision=lax.Precision.HIGHEST, preferred_element_type=jnp.float32,
-    )
-    grad_gain[...] = sums[:1] / gain[...]
-    keys_out[...] = keys[...]
-    outer_out[...] = outer[...]
-    mom_out[...] = mom[...]
-
-
-def gradients(act, back, weight, gain, keys, outer, mom):
-    seq, feats = act.shape
-    width = back.shape[1]
-    tiles = feats // 512
-
-    def rows_of(array):
-        return pl.BlockSpec((array.shape[0] // tiles, width), lambda i: (i, 0))
-
-    row = pl.BlockSpec((1, 512), lambda i: (0, i))
-    shape = jax.ShapeDtypeStruct
-    return pl.pallas_call(
-        gradient_kernel,
-        grid=(tiles,),
-        in_specs=[
-            pl.BlockSpec((seq, 512), lambda i: (0, i)),
-            pl.BlockSpec((seq, width), lambda i: (0, 0)),
-            rows_of(weight), row, rows_of(keys), rows_of(outer), rows_of(mom),
-        ],
-        out_specs=[rows_of(weight), row, rows_of(keys), rows_of(outer), rows_of(mom)],
-        out_shape=[
-            shape(weight.shape, jnp.bfloat16), shape((1, feats), jnp.float32),
-            shape(keys.shape, keys.dtype), shape(outer.shape, outer.dtype),
-            shape(mom.shape, mom.dtype),
-        ],
-        compiler_params=pltpu.CompilerParams(vmem_limit_bytes=32 * 1024 * 1024),
-    )(act, back, weight, gain, keys, outer, mom)
-
-
 def body(hidden, gain, doc_ids, cotangent, pseudo_grad, outer_weight, momentum):
     gain_row = gain.astype(jnp.float32)[None, :]
     weight, new_outer, new_momentum, act, back, keys = exchange(
         pseudo_grad[0], outer_weight, momentum, hidden[0], cotangent[0], doc_ids, gain_row
     )
-    grad_weight, grad_gain, keys, new_outer, new_momentum = gradients(
-        act, back, weight.reshape(-1, weight.shape[2]), gain_row, keys, new_outer, new_momentum
-    )
+    weight = weight.reshape(-1, weight.shape[2])
+    grad_weight = lax.dot_general(
+        act, back, (((0,), (0,)), ((), ())), preferred_element_type=jnp.float32
+    ).astype(jnp.bfloat16)
+    hidden_grad = lax.dot_general(
+        back, weight, (((1,), (1,)), ((), ())), preferred_element_type=jnp.float32
+    )
+    grad_gain = jnp.sum(hidden_grad * act.astype(jnp.float32), axis=0, keepdims=True) / gain_row
     return keys[None], grad_weight[None], grad_gain, new_outer, new_momentum
 
 

time: 103 us -> 94.5 us (0.917)
  Pallas kernels: 92 us -> 81 us
  matrix products: 0 us -> 7.68 us
  local copies, waits for them, and re-layouts: 7.71 us -> 2.27 us
    pallas_call x1 -> x0, Pallas kernels: 11 us -> none  [gradients(): pl.pallas_call(gradient_kernel, grid=(tiles,), in_specs=[pl.BlockSpec((se...]
    dot_general x0 -> x2, matrix products: none -> 7.68 us  [the longest x1 4.38 us: body(): lax.dot_general(back, weight, (((1,), (1,)), ((), ())), preferred_element...]
    unnamed x14 -> x15, local copies, waits for them, and re-layouts: 7.71 us -> 2.27 us
    convert_element_type x0 -> x1, other arithmetic: none -> 1.31 us  [body(): gain_row = gain.astype(jnp.float32)[None, :]]
    broadcast_in_dim x1 -> x0, other arithmetic: 1.3 us -> none  [body(): gain_row = gain.astype(jnp.float32)[None, :]]
where the time goes in v3:
time: 94.5 us; the launch traced here: 93.6 us
  Pallas kernels  81 us (86%)
  matrix products  7.68 us (8%)
  local copies, waits for them, and re-layouts  2.27 us (2%)
  other arithmetic  1.92 us (2%)
    pallas_call x1, Pallas kernels, exchange(): pl.pallas_call(functools.partial(exchange_kernel, islands, ways, stages,...  81 us
    dot_general x1, matrix products, body(): lax.dot_general(back, weight, (((1,), (1,)), ((), ())), preferred_element...  4.38 us
    dot_general x1, matrix products, body(): lax.dot_general(act, back, (((0,), (0,)), ((), ())), preferred_element_ty...  3.3 us
    unnamed x15, local copies, waits for them, and re-layouts  2.27 us

profile of v3, /device:TPU:0, one launch (start us, length us, event | category | flops | bytes accessed | tf_op | source)
XLA Modules:
  0.0 93.6 jit_solution(10372217212184304699)
XLA Ops:
  0.6 1.3 %convert_element_type.9 = f32[4096]{0:T(1024)} convert(bf16[4096]{0:T(1024)(128)(2,1)} %param.8) | non-fusion elementwise | flops 4096 | bytes 24576 | tf_op jit(solution)/shard_map/convert_element_type | solution.py:335
  1.9 81.0 %shard_map.110 = (bf16[16,256,512]{2,1,0:T(8,128)(2,1)}, f32[256,512]{1,0:T(8,128)}, f32[256,512]{1,0:T(8,128)}, bf16[256,4096]{1,0:T(8,128)(2,1)}, bf16[256,512]{1,0:T(8,128)(2,1)}, /*index=5*/bf16[128,512]{1,0:T(8,128)(2,1)}) custom-call(bf16[8,2,256,512]{3,2,1,0:T(8,128)(2,1)} %bitcast.13, f32[256,512]{1,0:T(8,128)} %refs_1_.1, f32[256,512]{1,0:T(8,128)} %refs_2_.1, ...), custom_call_target="tpu_custom_call" | custom-call | tf_op jit(solution)/shard_map/pallas_call | solution.py:302
  83.0 0.0 copy-start.5
  83.0 0.0 copy-start
  83.0 0.0 copy-start.3
  83.0 4.4 %fusion.1 = f32[4096]{0:T(1024)S(1)} fusion(bf16[256,4096]{1,0:T(8,128)(2,1)} %get-tuple-element.12, bf16[256,512]{1,0:T(8,128)(2,1)} %get-tuple-element.13, bf16[4096,512]{1,0:T(8,128)(2,1)} %bitcast.19), kind=kOutput, calls=%fused_computation.3 | convolution fusion | flops 1076883456 | bytes 6569984 | tf_op jit(solution)/shard_map/dot_general | solution.py:343
  87.4 0.0 copy-done.5
  87.4 0.0 copy-start.4
  87.4 0.0 copy-start.2
  87.4 0.6 convert_divide_fusion
  88.0 0.0 copy-done
  88.0 0.0 copy-done.3
  88.0 0.0 copy-start.1
  88.0 3.3 %fusion = bf16[1,4096,512]{2,1,0:T(8,128)(2,1)} fusion(bf16[256,4096]{1,0:T(8,128)(2,1)S(1)} %copy-done, bf16[256,512]{1,0:T(8,128)(2,1)S(1)} %copy-done.3), kind=kOutput, calls=%fused_computation.1 | convolution fusion | flops 1075838976 | bytes 6553600 | tf_op jit(solution)/shard_map/dot_general | solution.py:340
  91.3 0.0 copy-done.4
  91.3 0.7 copy.15
  92.0 0.0 copy-done.2
  92.0 0.8 copy.16
  92.8 0.0 copy-done.1
  92.8 0.8 copy.17
Async XLA Ops:
  83.0 4.4 %copy-start.5 = (bf16[4096]{0:T(1024)(128)(2,1)S(1)}, bf16[4096]{0:T(1024)(128)(2,1)}, u32[]{:S(2)}) copy-start(bf16[4096]{0:T(1024)(128)(2,1)} %param.8) | copy-start | bytes 24580
  83.0 5.1 %copy-start = (bf16[256,4096]{1,0:T(8,128)(2,1)S(1)}, bf16[256,4096]{1,0:T(8,128)(2,1)}, u32[]{:S(2)}) copy-start(bf16[256,4096]{1,0:T(8,128)(2,1)} %get-tuple-element.12) | copy-start | bytes 6291460
  83.0 5.0 %copy-start.3 = (bf16[256,512]{1,0:T(8,128)(2,1)S(1)}, bf16[256,512]{1,0:T(8,128)(2,1)}, u32[]{:S(2)}) copy-start(bf16[256,512]{1,0:T(8,128)(2,1)} %get-tuple-element.13) | copy-start | bytes 786436
  87.4 4.0 %copy-start.4 = (bf16[128,512]{1,0:T(8,128)(2,1)S(1)}, bf16[128,512]{1,0:T(8,128)(2,1)}, u32[]{:S(2)}) copy-start(bf16[128,512]{1,0:T(8,128)(2,1)} %get-tuple-element.11) | copy-start | bytes 393220
  87.4 4.6 %copy-start.2 = (f32[256,512]{1,0:T(8,128)S(1)}, f32[256,512]{1,0:T(8,128)}, u32[]{:S(2)}) copy-start(f32[256,512]{1,0:T(8,128)} %get-tuple-element.25) | copy-start | bytes 1572868
  88.0 4.8 %copy-start.1 = (f32[256,512]{1,0:T(8,128)S(1)}, f32[256,512]{1,0:T(8,128)}, u32[]{:S(2)}) copy-start(f32[256,512]{1,0:T(8,128)} %get-tuple-element.26) | copy-start | bytes 1572868

commit v4 on v3

--- a/solution.py
+++ b/solution.py
@@ -246,9 +246,9 @@
                 if tick == 1 and c == 0:
                     norms()
             elif stages <= k < 2 * stages:
-                if work:
+                gather_stage(2 * stages - 1 - k, c)
+                if work and 2 * stages - 1 - k <= 2:
                     work.pop(0)()
-                gather_stage(2 * stages - 1 - k, c)
 
     while work:
         work.pop(0)()

time: 94.5 us -> 95.9 us (1.015)
  Pallas kernels: 81 us -> 82.5 us
    pallas_call x1, Pallas kernels: 81 us -> 82.5 us  [exchange(): pl.pallas_call(functools.partial(exchange_kernel, islands, ways, stages,...]
where the time goes in v4:
time: 95.9 us; the launch traced here: 95 us
  Pallas kernels  82.5 us (86%)
  matrix products  7.69 us (8%)
  local copies, waits for them, and re-layouts  2.27 us (2%)
  other arithmetic  1.92 us (2%)
    pallas_call x1, Pallas kernels, exchange(): pl.pallas_call(functools.partial(exchange_kernel, islands, ways, stages,...  82.5 us
    dot_general x1, matrix products, body(): lax.dot_general(back, weight, (((1,), (1,)), ((), ())), preferred_element...  4.38 us
    dot_general x1, matrix products, body(): lax.dot_general(act, back, (((0,), (0,)), ((), ())), preferred_element_ty...  3.3 us
    unnamed x15, local copies, waits for them, and re-layouts  2.27 us

profile of v4, /device:TPU:0, one launch (start us, length us, event | category | flops | bytes accessed | tf_op | source)
XLA Modules:
  0.0 95.0 jit_solution(3503700610332004120)
XLA Ops:
  0.6 1.3 %convert_element_type.9 = f32[4096]{0:T(1024)} convert(bf16[4096]{0:T(1024)(128)(2,1)} %param.8) | non-fusion elementwise | flops 4096 | bytes 24576 | tf_op jit(solution)/shard_map/convert_element_type | solution.py:335
  1.9 82.5 %shard_map.110 = (bf16[16,256,512]{2,1,0:T(8,128)(2,1)}, f32[256,512]{1,0:T(8,128)}, f32[256,512]{1,0:T(8,128)}, bf16[256,4096]{1,0:T(8,128)(2,1)}, bf16[256,512]{1,0:T(8,128)(2,1)}, /*index=5*/bf16[128,512]{1,0:T(8,128)(2,1)}) custom-call(bf16[8,2,256,512]{3,2,1,0:T(8,128)(2,1)} %bitcast.13, f32[256,512]{1,0:T(8,128)} %refs_1_.1, f32[256,512]{1,0:T(8,128)} %refs_2_.1, ...), custom_call_target="tpu_custom_call" | custom-call | tf_op jit(solution)/shard_map/pallas_call | solution.py:302
  84.4 0.0 copy-start.5
  84.4 0.0 copy-start
  84.4 0.0 copy-start.3
  84.4 4.4 %fusion.1 = f32[4096]{0:T(1024)S(1)} fusion(bf16[256,4096]{1,0:T(8,128)(2,1)} %get-tuple-element.12, bf16[256,512]{1,0:T(8,128)(2,1)} %get-tuple-element.13, bf16[4096,512]{1,0:T(8,128)(2,1)} %bitcast.19), kind=kOutput, calls=%fused_computation.3 | convolution fusion | flops 1076883456 | bytes 6569984 | tf_op jit(solution)/shard_map/dot_general | solution.py:343
  88.8 0.0 copy-done.5
  88.8 0.0 copy-start.4
  88.8 0.0 copy-start.2
  88.9 0.6 convert_divide_fusion
  89.5 0.0 copy-done
  89.5 0.0 copy-done.3
  89.5 0.0 copy-start.1
  89.5 3.3 %fusion = bf16[1,4096,512]{2,1,0:T(8,128)(2,1)} fusion(bf16[256,4096]{1,0:T(8,128)(2,1)S(1)} %copy-done, bf16[256,512]{1,0:T(8,128)(2,1)S(1)} %copy-done.3), kind=kOutput, calls=%fused_computation.1 | convolution fusion | flops 1075838976 | bytes 6553600 | tf_op jit(solution)/shard_map/dot_general | solution.py:340
  92.8 0.0 copy-done.4
  92.8 0.7 copy.15
  93.4 0.0 copy-done.2
  93.5 0.8 copy.16
  94.2 0.0 copy-done.1
  94.2 0.8 copy.17
Async XLA Ops:
  84.4 4.4 %copy-start.5 = (bf16[4096]{0:T(1024)(128)(2,1)S(1)}, bf16[4096]{0:T(1024)(128)(2,1)}, u32[]{:S(2)}) copy-start(bf16[4096]{0:T(1024)(128)(2,1)} %param.8) | copy-start | bytes 24580
  84.4 5.1 %copy-start = (bf16[256,4096]{1,0:T(8,128)(2,1)S(1)}, bf16[256,4096]{1,0:T(8,128)(2,1)}, u32[]{:S(2)}) copy-start(bf16[256,4096]{1,0:T(8,128)(2,1)} %get-tuple-element.12) | copy-start | bytes 6291460
  84.4 5.1 %copy-start.3 = (bf16[256,512]{1,0:T(8,128)(2,1)S(1)}, bf16[256,512]{1,0:T(8,128)(2,1)}, u32[]{:S(2)}) copy-start(bf16[256,512]{1,0:T(8,128)(2,1)} %get-tuple-element.13) | copy-start | bytes 786436
  88.8 4.0 %copy-start.4 = (bf16[128,512]{1,0:T(8,128)(2,1)S(1)}, bf16[128,512]{1,0:T(8,128)(2,1)}, u32[]{:S(2)}) copy-start(bf16[128,512]{1,0:T(8,128)(2,1)} %get-tuple-element.11) | copy-start | bytes 393220
  88.8 4.6 %copy-start.2 = (f32[256,512]{1,0:T(8,128)S(1)}, f32[256,512]{1,0:T(8,128)}, u32[]{:S(2)}) copy-start(f32[256,512]{1,0:T(8,128)} %get-tuple-element.25) | copy-start | bytes 1572868
  89.5 4.8 %copy-start.1 = (f32[256,512]{1,0:T(8,128)S(1)}, f32[256,512]{1,0:T(8,128)}, u32[]{:S(2)}) copy-start(f32[256,512]{1,0:T(8,128)} %get-tuple-element.26) | copy-start | bytes 1572868
